TPU v7x, 32 devices: a whole 2x2x4 slice. The times are simulated.
32 devices in a mesh: grp: 2 (over y), ctx: 4 (over z), exp: 2 (over x), tp: 2 (over core).
Axes of the slice: x: 2, y: 2, z: 4, core: 2. Of those that a mesh axis runs over, the one named last changes fastest.
Arguments:
- queries: bfloat16 [512, 6144], P(('grp', 'ctx'), ('exp', 'tp')), parts along dimension 0, may hold values from -16 to 16
- rotated_key_heads: bfloat16 [512, 1024], P(('grp', 'ctx'), ('exp', 'tp')), parts along dimension 0, may hold values from -16 to 16
- stored_value_heads: bfloat16 [512, 1024], P(('grp', 'ctx'), ('exp', 'tp')), parts along dimension 0, may hold values from -6 to 6
- block_order: int32 [16], P('grp'), parts along dimension 0, may hold values from 0 to 7, each once
- residual: bfloat16 [512, 6144], P(('grp', 'ctx', 'exp', 'tp')), parts along dimension 0, may hold values from -10 to 10
- out_weight: bfloat16 [6144, 6144], P(('exp', 'tp'), 'ctx'), may hold values from -0.5 to 0.5
- norm_gain: bfloat16 [6144], replicated, may hold values from 0.099609375 to 1.8984375
- expert_ids: int32 [512, 2], P(('grp', 'ctx', 'exp', 'tp')), parts along dimension 0, may hold values from 0 to 3, all different within a row; in each aligned block of 16 rows (0 to 15, 16 to 31, ...) at most 12 rows name the same one
- gate_logits: float32 [512, 2], P(('grp', 'ctx', 'exp', 'tp')), parts along dimension 0, may hold values from -6 to 6
- w_gate: bfloat16 [4, 6144, 8192], P('exp', None, ('ctx', 'tp')), may hold values from -0.078125 to 0.078125
- w_up: bfloat16 [4, 6144, 8192], P('exp', None, ('ctx', 'tp')), may hold values from -0.078125 to 0.078125
- w_down: bfloat16 [4, 8192, 6144], P('exp', ('ctx', 'tp')), may hold values from -0.0625 to 0.0625
Outputs:
- layer_out: bfloat16 [512, 6144], P(('grp', 'ctx', 'exp', 'tp')), parts along dimension 0
There are 2 independent parts, one for each index of `grp`. A program takes and returns all parts, laid end to end along the dimension named above; an argument that names none is the same for every part. Nothing has to cross between parts.
Inputs may be any that keep to these rules, and one draw needn't show every extreme that they name: `expert_ids`: in the rows of one device (aligned blocks of 16 rows) each expert is named by at most 12 rows, a bound that some block reaches; the two ids of a row differ. A permutation: stored block b holds the positions block_order[b] * 32 onward, in order.
All inputs are finite; a program needn't handle non-finite values.
Results may differ from a plain program's by a relative error of at most 0.014.
Values may be sent and summed in bfloat16 or wider, within the bound.
A program may use at most 256 MiB of HBM per device.

v0:
```python
import math

import jax
import jax.numpy as jnp
from jax import lax
from jax.sharding import PartitionSpec as P

HEAD_SIZE = 128
EXPERTS = 4
BLOCK = 32


neg_large = -1e30


def positions(block_order, row_index):
    block_index = row_index // BLOCK
    match_table = block_index[:, None] == jnp.arange(block_order.shape[0], dtype=jnp.int32)[None, :]
    return (
        jnp.sum(jnp.where(match_table, block_order[None, :], 0), axis=1) * BLOCK + row_index % BLOCK
    )


def attend(queries, rotated_key_heads, stored_value_heads, block_order):
    span_rows = queries.shape[0]
    kv_local = rotated_key_heads.shape[1] // HEAD_SIZE
    query_group_width = queries.shape[1] // rotated_key_heads.shape[1]
    query_head_table = queries.reshape(span_rows, kv_local, query_group_width, HEAD_SIZE)
    query_pos = positions(
        block_order, lax.axis_index("ctx") * span_rows + jnp.arange(span_rows, dtype=jnp.int32)
    )
    score_scale = 1.0 / math.sqrt(HEAD_SIZE)
    key_part = lax.all_gather(rotated_key_heads, "ctx", axis=0, tiled=True)
    value_part = lax.all_gather(stored_value_heads, "ctx", axis=0, tiled=True)
    piece_rows = key_part.shape[0]
    key_pos = positions(block_order, jnp.arange(piece_rows, dtype=jnp.int32))
    allowed = key_pos[None, :] <= query_pos[:, None]
    key_head_table = key_part.reshape(piece_rows, kv_local, HEAD_SIZE)
    value_head_table = value_part.reshape(piece_rows, kv_local, HEAD_SIZE).astype(jnp.float32)
    scores = (
        jnp.einsum(
            "tkgd,skd->kgts", query_head_table, key_head_table, preferred_element_type=jnp.float32
        )
        * score_scale
    )
    scores = jnp.where(allowed, scores, neg_large)
    peak_score = jnp.full((kv_local, query_group_width, span_rows), neg_large, jnp.float32)
    new_peak = jnp.maximum(peak_score, jnp.max(scores, axis=-1))
    weights = jnp.where(allowed, jnp.exp(scores - new_peak[..., None]), 0.0)
    weight_total = jnp.sum(weights, axis=-1)
    summed = jnp.einsum(
        "kgts,skd->kgtd", weights, value_head_table, precision=lax.Precision.HIGHEST
    )
    peak_score, weight_total, summed = (new_peak, weight_total, summed)
    mixed_heads = summed / weight_total[..., None]
    return jnp.transpose(mixed_heads, (2, 0, 1, 3)).reshape(span_rows, -1).astype(jnp.bfloat16)


def expert_apply(slot_rows, gate_w, up_w, down_w):
    gate_val = jnp.dot(slot_rows, gate_w, preferred_element_type=jnp.float32)
    up_val = jnp.dot(slot_rows, up_w, preferred_element_type=jnp.float32)
    active = (jax.nn.silu(gate_val) * up_val).astype(jnp.bfloat16)
    return jnp.dot(active, down_w, preferred_element_type=jnp.float32)


def shards(
    queries,
    rotated_key_heads,
    stored_value_heads,
    block_order,
    residual,
    out_weight,
    norm_gain,
    expert_ids,
    gate_logits,
    w_gate,
    w_up,
    w_down,
):
    attended = attend(queries, rotated_key_heads, stored_value_heads, block_order)
    tok_rows = residual.shape[0]
    head_terms = jnp.dot(
        attended,
        lax.all_gather(out_weight, "ctx", axis=1, tiled=True),
        preferred_element_type=jnp.float32,
    )
    projected = lax.psum_scatter(
        head_terms.astype(jnp.bfloat16), ("exp", "tp"), scatter_dimension=0, tiled=True
    ).astype(jnp.float32)
    hidden_state = (residual.astype(jnp.float32) + projected).astype(jnp.bfloat16)
    state_f32 = hidden_state.astype(jnp.float32)
    normed = (
        state_f32
        * lax.rsqrt(jnp.mean(state_f32 * state_f32, axis=-1, keepdims=True) + 1e-05)
        * norm_gain.astype(jnp.float32)
    ).astype(jnp.bfloat16)
    capacity = 3 * tok_rows // 4
    flat_ids = expert_ids.reshape(-1)
    one_hot = (flat_ids[:, None] == jnp.arange(EXPERTS, dtype=jnp.int32)[None, :]).astype(jnp.int32)
    earlier = jnp.cumsum(one_hot, axis=0) - one_hot
    slot_index = jnp.sum(earlier * one_hot, axis=1)
    target = flat_ids * capacity + slot_index
    slot_ids = jnp.arange(EXPERTS * capacity, dtype=jnp.int32)
    picker = jnp.any(
        slot_ids[:, None, None] == target.reshape(tok_rows, -1)[None, :, :], axis=2
    ).astype(jnp.bfloat16)
    outgoing = jnp.dot(picker, normed, preferred_element_type=jnp.float32).astype(jnp.bfloat16)
    exp_count = lax.axis_size("exp")
    local_experts = EXPERTS // exp_count
    outgoing = outgoing.reshape(exp_count, local_experts, capacity, -1)
    arrived = lax.all_to_all(outgoing, "exp", split_axis=0, concat_axis=0, tiled=True)
    fragment = lax.all_gather(arrived[None], ("ctx", "tp"), axis=0, tiled=True)
    outputs = []
    for local_index in range(local_experts):
        slot_rows = fragment[:, :, local_index].reshape(-1, fragment.shape[-1])
        result = expert_apply(
            slot_rows, w_gate[local_index], w_up[local_index], w_down[local_index]
        )
        outputs.append(result.reshape(fragment.shape[0], fragment.shape[1], fragment.shape[3], -1))
    partials = jnp.stack(outputs, axis=2)
    combined = lax.psum_scatter(
        partials.astype(jnp.bfloat16), ("ctx", "tp"), scatter_dimension=0, tiled=True
    ).astype(jnp.float32)
    returned = lax.all_to_all(
        combined[0].astype(jnp.bfloat16), "exp", split_axis=0, concat_axis=1, tiled=True
    )
    back_rows = returned.reshape(EXPERTS * capacity, -1)
    picked = back_rows[target].astype(jnp.float32).reshape(tok_rows, 2, -1)
    first_weight = jax.nn.sigmoid(gate_logits[:, 0] - gate_logits[:, 1])
    second_weight = jax.nn.sigmoid(gate_logits[:, 1] - gate_logits[:, 0])
    mixture = first_weight[:, None] * picked[:, 0] + second_weight[:, None] * picked[:, 1]
    return (hidden_state.astype(jnp.float32) + mixture).astype(jnp.bfloat16)


def solution(mesh):
    placed = (
        P(("grp", "ctx"), ("exp", "tp")),
        P(("grp", "ctx"), ("exp", "tp")),
        P(("grp", "ctx"), ("exp", "tp")),
        P("grp"),
        P(("grp", "ctx", "exp", "tp"), None),
        P(("exp", "tp"), "ctx"),
        P(),
        P(("grp", "ctx", "exp", "tp"), None),
        P(("grp", "ctx", "exp", "tp"), None),
        P("exp", None, ("ctx", "tp")),
        P("exp", None, ("ctx", "tp")),
        P("exp", ("ctx", "tp"), None),
    )
    return jax.shard_map(
        shards,
        mesh=mesh,
        in_specs=placed,
        out_specs=P(("grp", "ctx", "exp", "tp"), None),
        check_vma=False,
    )
```

profile of v0, /device:TPU:0, one launch (start us, length us, event | category | flops | bytes accessed | tf_op | source)
XLA Modules:
  0.0 659.9 jit_solution(1978305467222700151)
XLA Ops:
  7.3 15.3 %all_gather.12 = bf16[256,256]{1,0:T(8,128)(2,1)S(1)} all-gather(bf16[64,256]{1,0:T(8,128)(2,1)} %param.13), channel_id=1, replica_groups=mesh['grp'=2,'ctx'=4,'exp'=2,'tp'=2] {'ctx'}, dimensions={0}, use_global_device_ids=true | all-gather | bytes 163840 | tf_op jit(solution)/shard_map/all_gather | solution.py:33
  24.0 33.8 %all_gather.13 = bf16[256,256]{1,0:T(8,128)(2,1)S(1)} all-gather(bf16[64,256]{1,0:T(8,128)(2,1)} %param.14), channel_id=1, replica_groups=mesh['grp'=2,'ctx'=4,'exp'=2,'tp'=2] {'ctx'}, dimensions={0}, use_global_device_ids=true | all-gather | bytes 163840 | tf_op jit(solution)/shard_map/all_gather | solution.py:34
  61.2 274.6 %all-gather.4.cloned.1.call-done = bf16[1536,6144]{1,0:T(8,128)(2,1)} async-done(((bf16[1536,1536]{1,0:T(8,128)(2,1)}), bf16[1536,6144]{1,0:T(8,128)(2,1)}) %all-gather.4.cloned.1.call-update) | async-done | bytes 18874384 | tf_op jit(solution)/shard_map/all_gather | solution.py:84
  335.8 10.7 %convolution_convert_fusion = bf16[64,6144]{1,0:T(8,128)(2,1)} fusion(bf16[64,1536]{1,0:T(8,128)(2,1)S(1)} %convert_element_type.60, bf16[1536,6144]{1,0:T(8,128)(2,1)} %all-gather.4.cloned.1.call-done), kind=kOutput, calls=%fused_computation.23 | convolution fusion | flops 1208352768 | bytes 19857408 | tf_op jit(solution)/shard_map/dot_general | solution.py:82
  347.3 21.2 %reduce-scatter.2.cloned.1.call-done = bf16[16,6144]{1,0:T(8,128)(2,1)} async-done(((bf16[64,6144]{1,0:T(8,128)(2,1)}), bf16[16,6144]{1,0:T(8,128)(2,1)}) %reduce-scatter.2.cloned.1.call-update) | async-done | bytes 196624 | tf_op jit(solution)/shard_map/reduce_scatter | solution.py:87
  369.7 1.3 convolution_convert_fusion.1
  371.7 12.1 %all_to_all.14 = bf16[2,2,12,6144]{3,1,2,0:T(2,128)(2,1)} all-to-all(bf16[2,2,12,6144]{3,1,2,0:T(2,128)(2,1)S(1)} %copy.53), channel_id=1, replica_groups=mesh['grp'=2,'ctx'=4,'exp'=2,'tp'=2] {'exp'}, dimensions={0} | all-to-all | bytes 1179648 | tf_op jit(solution)/shard_map/all_to_all | solution.py:111
  384.0 51.6 %all-gather.6.cloned.1.call-done = bf16[16,2,12,6144]{3,1,2,0:T(2,128)(2,1)} async-done(((bf16[2,2,12,6144]{3,1,2,0:T(2,128)(2,1)}), bf16[16,2,12,6144]{3,1,2,0:T(2,128)(2,1)}) %all-gather.6.cloned.1.call-update) | async-done | bytes 4718608 | tf_op jit(solution)/shard_map/all_gather | solution.py:112
  435.7 24.1 %slice_reduce_fusion.1 = (bf16[8,2,12,6144]{3,2,1,0:T(8,128)(2,1)}, bf16[8,2,12,6144]{3,2,1,0:T(8,128)(2,1)S(1)}) fusion(bf16[8,2,2,12,6144]{4,2,3,1,0:T(2,128)(2,1)} %bitcast.106), kind=kLoop, calls=%fused_computation.27 | loop fusion | bytes 9437184 | tf_op jit(solution)/shard_map/slice | solution.py:115
  459.8 4.2 reshape_squeeze.6
  464.0 7.9 %fusion.10 = f32[192,1024]{1,0:T(8,128)S(1)} fusion(bf16[192,6144]{1,0:T(8,128)(2,1)} %reshape_squeeze.6, bf16[2,6144,1024]{2,1,0:T(8,128)(2,1)} %param.21), kind=kOutput, calls=%fused_computation.11 | convolution fusion | flops 2415919104 | bytes 15728640 | tf_op jit(solution)/shard_map/dot_general | solution.py:60
  471.9 8.0 %fusion.41 = bf16[192,1024]{1,0:T(8,128)(2,1)} fusion(bf16[192,6144]{1,0:T(8,128)(2,1)S(1)} %copy-done, bf16[2,6144,1024]{2,1,0:T(8,128)(2,1)} %param.22, f32[192,1024]{1,0:T(8,128)S(1)} %fusion.10), kind=kOutput, calls=%fused_computation.34 | convolution fusion | flops 2417098752 | bytes 16121856 | tf_op jit(solution)/shard_map/dot_general | solution.py:61
  479.9 1.9 reshape.156
  481.8 2.1 reshape_squeeze.7
  483.9 8.3 %fusion.6 = f32[192,1024]{1,0:T(8,128)S(1)} fusion(bf16[192,6144]{1,0:T(8,128)(2,1)} %reshape_squeeze.7, bf16[2,6144,1024]{2,1,0:T(8,128)(2,1)} %param.21), kind=kOutput, calls=%fused_computation.7 | convolution fusion | flops 2415919104 | bytes 15728640 | tf_op jit(solution)/shard_map/dot_general | solution.py:60
  492.3 7.3 %fusion.38 = bf16[192,1024]{1,0:T(8,128)(2,1)S(1)} fusion(bf16[192,6144]{1,0:T(8,128)(2,1)S(1)} %copy-done.1, bf16[2,6144,1024]{2,1,0:T(8,128)(2,1)} %param.22, f32[192,1024]{1,0:T(8,128)S(1)} %fusion.6), kind=kOutput, calls=%fused_computation.33 | convolution fusion | flops 2417098752 | bytes 16121856 | tf_op jit(solution)/shard_map/dot_general | solution.py:61
  499.7 8.0 %fusion.27 = bf16[8,2,1,12,6144]{4,3,1,0,2:T(8,128)(2,1)S(1)} fusion(bf16[8,2,12,1024]{3,2,1,0:T(8,128)(2,1)S(1)} %copy-done.4, bf16[2,1024,6144]{2,1,0:T(8,128)(2,1)} %param.23), kind=kOutput, calls=%fused_computation.22 | convolution fusion | flops 2417098752 | bytes 15335424 | tf_op jit(solution)/shard_map/dot_general | solution.py:63
  507.7 8.0 %fusion.24 = bf16[8,2,1,12,6144]{4,3,1,0,2:T(8,128)(2,1)S(1)} fusion(bf16[8,2,12,1024]{3,2,1,0:T(8,128)(2,1)S(1)} %reshape.157, bf16[2,1024,6144]{2,1,0:T(8,128)(2,1)} %param.23), kind=kOutput, calls=%fused_computation.21 | convolution fusion | flops 2417098752 | bytes 15335424 | tf_op jit(solution)/shard_map/dot_general | solution.py:63
  515.7 3.5 pad_maximum_fusion
  519.3 10.2 %copy.56 = bf16[8,2,2,12,6144]{4,2,3,1,0:T(2,128)(2,1)} copy(bf16[8,2,2,12,6144]{4,3,1,0,2:T(8,128)(2,1)} %pad_maximum_fusion) | data formatting | bytes 9437184 | tf_op jit(solution)/shard_map/stack | solution.py:120
  530.2 104.7 %all-reduce.3.cloned.1.call-done = bf16[8,2,2,12,6144]{4,2,3,1,0:T(2,128)(2,1)} async-done(((bf16[8,2,2,12,6144]{4,2,3,1,0:T(2,128)(2,1)}), bf16[8,2,2,12,6144]{4,2,3,1,0:T(2,128)(2,1)}) %all-reduce.3.cloned.1.call-update) | async-done | bytes 4718608
  634.8 3.0 dynamic-slice_bitcast_fusion
  637.8 3.5 all-to-all-start.1
  641.3 8.8 %all-to-all-done.1 = bf16[2,2,12,6144]{3,1,2,0:T(2,128)(2,1)S(1)} async-done(((bf16[2,2,12,6144]{3,1,2,0:T(2,128)(2,1)}), bf16[2,2,12,6144]{3,1,2,0:T(2,128)(2,1)S(1)}, u32[]{:S(2)}, u32[]{:S(2)}) %all-to-all-start.1) | async-done | bytes 589856 | tf_op jit(solution)/shard_map/all_to_all | solution.py:124
  (68 shorter events, 12.4 us)
Async XLA Ops:
  6.5 329.3 %all-gather.4.cloned.1.call-start = ((), (), s32[]{:S(2)}) async-start(), calls=%async_computation.3 | async-start | bytes 23592960 | tf_op jit(solution)/shard_map/all_gather | solution.py:84
  7.3 361.3 %reduce-scatter.2.cloned.1.call-start = ((), (), s32[]{:S(2)}) async-start(), calls=%async_computation.4 | async-start | bytes 983040 | tf_op jit(solution)/shard_map/reduce_scatter | solution.py:87
  61.1 285.4 %copy-start.6 = (s32[16,2]{0,1:T(2,128)S(1)}, s32[16,2]{0,1:T(2,128)}, u32[]{:S(2)}) copy-start(s32[16,2]{0,1:T(2,128)} %param.19) | copy-start | bytes 388
  61.2 286.1 %copy-start.5 = (bf16[6144]{0:T(1024)(128)(2,1)S(1)}, bf16[6144]{0:T(1024)(128)(2,1)}, u32[]{:S(2)}) copy-start(bf16[6144]{0:T(1024)(128)(2,1)} %param.18) | copy-start | bytes 36868
  61.2 307.4 %copy-start.2 = (bf16[16,6144]{1,0:T(8,128)(2,1)S(1)}, bf16[16,6144]{1,0:T(8,128)(2,1)}, u32[]{:S(2)}) copy-start(bf16[16,6144]{1,0:T(8,128)(2,1)} %param.16) | copy-start | bytes 589828
  346.5 89.2 %all-gather.6.cloned.1.call-start = ((), (), s32[]{:S(2)}) async-start(), calls=%async_computation.5 | async-start | bytes 5308416 | tf_op jit(solution)/shard_map/all_gather | solution.py:112
  383.8 251.0 %all-reduce.3.cloned.1.call-start = ((), (), s32[]{:S(2)}) async-start(), calls=%async_computation.6 | async-start | bytes 9437184
  464.0 7.9 %copy-start = (bf16[192,6144]{1,0:T(8,128)(2,1)S(1)}, bf16[192,6144]{1,0:T(8,128)(2,1)}, u32[]{:S(2)}) copy-start(bf16[192,6144]{1,0:T(8,128)(2,1)} %reshape_squeeze.6) | copy-start | bytes 7077892
  483.9 8.4 %copy-start.1 = (bf16[192,6144]{1,0:T(8,128)(2,1)S(1)}, bf16[192,6144]{1,0:T(8,128)(2,1)}, u32[]{:S(2)}) copy-start(bf16[192,6144]{1,0:T(8,128)(2,1)} %reshape_squeeze.7) | copy-start | bytes 7077892
  492.3 7.4 %copy-start.4 = (bf16[8,2,12,1024]{3,2,1,0:T(8,128)(2,1)S(1)}, bf16[8,2,12,1024]{3,2,1,0:T(8,128)(2,1)}, u32[]{:S(2)}) copy-start(bf16[8,2,12,1024]{3,2,1,0:T(8,128)(2,1)} %reshape.156) | copy-start | bytes 1179652
  519.3 10.3 %copy-start.8 = (u32[32]{0:T(128)S(1)}, u32[32]{0:T(128)}, u32[]{:S(2)}) copy-start(u32[32]{0:T(128)} %constant.93) | copy-start | bytes 388
  529.4 111.9 %copy-start.7 = (f32[16,2]{0,1:T(2,128)S(1)}, f32[16,2]{0,1:T(2,128)}, u32[]{:S(2)}) copy-start(f32[16,2]{0,1:T(2,128)} %param.20) | copy-start | bytes 388
  529.5 122.9 %copy-start.3 = (bf16[16,6144]{1,0:T(8,128)(2,1)S(1)}, bf16[16,6144]{1,0:T(8,128)(2,1)}, u32[]{:S(2)}) copy-start(bf16[16,6144]{1,0:T(8,128)(2,1)} %reduce-scatter.2.cloned.1.call-done) | copy-start | bytes 589828
  637.8 12.4 %all-to-all-start.1 = ((bf16[2,2,12,6144]{3,1,2,0:T(2,128)(2,1)}), bf16[2,2,12,6144]{3,1,2,0:T(2,128)(2,1)S(1)}, u32[]{:S(2)}, u32[]{:S(2)}) async-start(bf16[2,2,12,6144]{3,1,2,0:T(2,128)(2,1)} %dynamic-slice_bitcast_fusion), calls=%async_computation.2 | async-start | bytes 1179648 | tf_op jit(solution)/shard_map/all_to_all | solution.py:124
Sparse Core Ops, SparseCore 0:
  8.9 326.8 all-gather.3
  346.6 21.8 reduce-scatter.1
  383.9 51.7 all-gather.5
  529.6 105.1 all-reduce.2
where the time goes:
time: 661 us; the launch traced here: 660 us
  waiting for transfers between devices  462 us (70%)
  blocking collectives  61.1 us (9%)
  matrix products  60.4 us (9%)
  local copies, waits for them, and re-layouts  51.4 us (8%)
  between operations  13.5 us (2%)
  other arithmetic  7.96 us (1%)
    all_gather x1, waiting for transfers between devices, shards(): lax.all_gather(out_weight, 'ctx', axis=1, tiled=True)  275 us
    unnamed x5, waiting for transfers between devices  105 us
    all_gather x1, waiting for transfers between devices, shards(): fragment = lax.all_gather(arrived[None], ('ctx', 'tp'), axis=0, tiled=True)  51.6 us
    all_gather x1, blocking collectives, attend(): value_part = lax.all_gather(stored_value_heads, 'ctx', axis=0, tiled=True)  33.8 us
    slice x1, local copies, waits for them, and re-layouts, shards(): slot_rows = fragment[:, :, local_index].reshape(-1, fragment.shape[-1])  24.1 us
    reduce_scatter x1, waiting for transfers between devices, shards(): lax.psum_scatter(head_terms.astype(jnp.bfloat16), ('exp', 'tp'), scatter_...  21.2 us
    dot_general x2, matrix products, expert_apply(): gate_val = jnp.dot(slot_rows, gate_w, preferred_element_type=jnp.float32)  16.3 us
    dot_general x2, matrix products, expert_apply(): return jnp.dot(active, down_w, preferred_element_type=jnp.float32)  16 us
  transfers between devices with their start and end apart: 5, of which 5 were waited for; matrix products, arithmetic and copies ran while one was open for 1% of the time, Pallas kernels for 0%

commit v1 on v0

v1 whole, which is shorter than its diff:
```python
import math

import jax
import jax.numpy as jnp
from jax import lax
from jax.sharding import PartitionSpec as P

HEAD_SIZE = 128
EXPERTS = 4
BLOCK = 32
NEG_LARGE = -1e30


def positions(block_order, rows):
    return (block_order[:, None] * BLOCK + jnp.arange(BLOCK, dtype=jnp.int32)[None, :]).reshape(rows)


def attend(queries, keys, values, block_order):
    rows = queries.shape[0]
    kv_local = keys.shape[1] // HEAD_SIZE
    group = queries.shape[1] // keys.shape[1]
    pos = positions(block_order, rows)
    allowed = pos[None, :] <= pos[:, None]
    scale = 1.0 / math.sqrt(HEAD_SIZE)
    heads = []
    for k in range(kv_local):
        key = keys[:, k * HEAD_SIZE : (k + 1) * HEAD_SIZE]
        value = values[:, k * HEAD_SIZE : (k + 1) * HEAD_SIZE]
        q = queries[:, k * group * HEAD_SIZE : (k + 1) * group * HEAD_SIZE].reshape(rows, group, HEAD_SIZE)
        scores = jnp.einsum("tgd,sd->gts", q, key, preferred_element_type=jnp.float32) * scale
        scores = jnp.where(allowed[None], scores, NEG_LARGE)
        weights = jnp.exp(scores - jnp.max(scores, axis=-1, keepdims=True))
        total = jnp.sum(weights, axis=-1, keepdims=True)
        mixed = jnp.einsum(
            "gts,sd->gtd", weights.astype(jnp.bfloat16), value, preferred_element_type=jnp.float32
        )
        heads.append(jnp.transpose((mixed / total).astype(jnp.bfloat16), (1, 0, 2)).reshape(rows, -1))
    return jnp.concatenate(heads, axis=1)


def shards(
    queries,
    rotated_key_heads,
    stored_value_heads,
    block_order,
    residual,
    out_weight,
    norm_gain,
    expert_ids,
    gate_logits,
    w_gate,
    w_up,
    w_down,
):
    ctx, exp, tp = (lax.axis_size(name) for name in ("ctx", "exp", "tp"))
    tok_rows, width = residual.shape
    local_experts = EXPERTS // exp
    all_axes = ("ctx", "exp", "tp")

    first = jax.nn.sigmoid(gate_logits[:, 0] - gate_logits[:, 1])
    second = jax.nn.sigmoid(gate_logits[:, 1] - gate_logits[:, 0])
    names = jnp.arange(EXPERTS, dtype=jnp.int32)[None, :]
    row_gates = first[:, None] * (expert_ids[:, :1] == names) + second[:, None] * (expert_ids[:, 1:] == names)
    gates = lax.all_gather(row_gates, all_axes, axis=0, tiled=True)

    qw, kw = queries.shape[1], rotated_key_heads.shape[1]
    own = jnp.concatenate([queries, rotated_key_heads, stored_value_heads], axis=1)
    qkv = lax.all_gather(own, "ctx", axis=0, tiled=True)
    attended = attend(qkv[:, :qw], qkv[:, qw : qw + kw], qkv[:, qw + kw :], block_order)
    part = jnp.dot(attended, out_weight, preferred_element_type=jnp.float32).astype(jnp.bfloat16)
    part = part.reshape(ctx, exp * tp, tok_rows, -1)
    part = lax.psum_scatter(part, ("exp", "tp"), scatter_dimension=1, tiled=True)
    part = part.reshape(ctx, tok_rows, -1)
    part = lax.all_to_all(part, "ctx", split_axis=0, concat_axis=0, tiled=True)
    projected = jnp.transpose(part, (1, 0, 2)).reshape(tok_rows, width).astype(jnp.float32)
    hidden_state = (residual.astype(jnp.float32) + projected).astype(jnp.bfloat16)
    state = hidden_state.astype(jnp.float32)
    normed = (
        state
        * lax.rsqrt(jnp.mean(state * state, axis=-1, keepdims=True) + 1e-05)
        * norm_gain.astype(jnp.float32)
    ).astype(jnp.bfloat16)

    rows = lax.all_gather(normed, all_axes, axis=0, tiled=True)
    base = lax.axis_index("exp") * local_experts
    actives = []
    gate_val = jnp.einsum("rd,edf->erf", rows, w_gate, preferred_element_type=jnp.float32)
    up_val = jnp.einsum("rd,edf->erf", rows, w_up, preferred_element_type=jnp.float32)
    local_gates = lax.dynamic_slice_in_dim(gates, base, local_experts, axis=1)
    active = (jax.nn.silu(gate_val) * up_val * local_gates.T[:, :, None]).astype(jnp.bfloat16)
    active = jnp.transpose(active, (1, 0, 2)).reshape(rows.shape[0], -1)
    sums = jnp.dot(active, w_down.reshape(-1, width), preferred_element_type=jnp.float32)
    mixture = lax.psum_scatter(sums.astype(jnp.bfloat16), all_axes, scatter_dimension=0, tiled=True)
    return (state + mixture.astype(jnp.float32)).astype(jnp.bfloat16)


def solution(mesh):
    placed = (
        P(("grp", "ctx"), ("exp", "tp")),
        P(("grp", "ctx"), ("exp", "tp")),
        P(("grp", "ctx"), ("exp", "tp")),
        P("grp"),
        P(("grp", "ctx", "exp", "tp"), None),
        P(("exp", "tp"), "ctx"),
        P(),
        P(("grp", "ctx", "exp", "tp"), None),
        P(("grp", "ctx", "exp", "tp"), None),
        P("exp", None, ("ctx", "tp")),
        P("exp", None, ("ctx", "tp")),
        P("exp", ("ctx", "tp"), None),
    )
    return jax.shard_map(
        shards,
        mesh=mesh,
        in_specs=placed,
        out_specs=P(("grp", "ctx", "exp", "tp"), None),
        check_vma=False,
    )
```

time: 661 us -> 256 us (0.39)
  waiting for transfers between devices: 462 us -> 160 us
  local copies, waits for them, and re-layouts: 51.4 us -> 4.7 us
  blocking collectives: 61.1 us -> 19.4 us
  matrix products: 60.4 us -> 47.2 us
    all_gather x2, waiting for transfers between devices: 326 us -> 55 us  [the longest x1 30.4 us: shards(): qkv = lax.all_gather(own, 'ctx', axis=0, tiled=True)]
    unnamed x5, waiting for transfers between devices: 105 us -> 33.7 us
    reduce_scatter x1, waiting for transfers between devices: 21.2 us -> 65.2 us  [shards(): lax.psum_scatter(sums.astype(jnp.bfloat16), all_axes, scatter_dimension=0...]
    all_gather x2 -> x1, blocking collectives: 49 us -> 19.4 us  [shards(): gates = lax.all_gather(row_gates, all_axes, axis=0, tiled=True)]
    slice x2 -> x3, local copies, waits for them, and re-layouts: 24.7 us -> 1.51 us  [attend(): queries[:, k * group * HEAD_SIZE:(k + 1) * group * HEAD_SIZE]]
    another operation x5 -> x0, local copies, waits for them, and re-layouts: 18.5 us -> none  [the longest x1 10.2 us: shards(): partials = jnp.stack(outputs, axis=2)]
    dot_general x10 -> x7, matrix products: 60.4 us -> 47.2 us  [the longest x1 22.8 us: shards(): jnp.dot(active, w_down.reshape(-1, width), preferred_element_type=jnp.flo...]
    all_to_all x1 -> x0, blocking collectives: 12.1 us -> none  [shards(): lax.all_to_all(outgoing, 'exp', split_axis=0, concat_axis=0, tiled=True)]
where the time goes in v1:
time: 256 us; the launch traced here: 255 us
  waiting for transfers between devices  160 us (62%)
  matrix products  47.2 us (18%)
  blocking collectives  19.4 us (8%)
  between operations  13.3 us (5%)
  other arithmetic  5.68 us (2%)
  local copies, waits for them, and re-layouts  4.7 us (2%)
  starting transfers between devices  4.69 us (2%)
    reduce_scatter x1, waiting for transfers between devices, shards(): lax.psum_scatter(sums.astype(jnp.bfloat16), all_axes, scatter_dimension=0...  65.2 us
    unnamed x5, waiting for transfers between devices  33.7 us
    all_gather x1, waiting for transfers between devices, shards(): qkv = lax.all_gather(own, 'ctx', axis=0, tiled=True)  30.4 us
    all_gather x1, waiting for transfers between devices, shards(): rows = lax.all_gather(normed, all_axes, axis=0, tiled=True)  24.7 us
    dot_general x1, matrix products, shards(): jnp.dot(active, w_down.reshape(-1, width), preferred_element_type=jnp.flo...  22.8 us
    all_gather x1, blocking collectives, shards(): gates = lax.all_gather(row_gates, all_axes, axis=0, tiled=True)  19.4 us
    dot_general x1, matrix products, shards(): jnp.einsum('rd,edf->erf', rows, w_gate, preferred_element_type=jnp.float32)  16.9 us
    all_to_all x1, waiting for transfers between devices, shards(): part = lax.all_to_all(part, 'ctx', split_axis=0, concat_axis=0, tiled=True)  6.44 us
  transfers between devices with their start and end apart: 5, of which 5 were waited for; matrix products, arithmetic and copies ran while one was open for 1% of the time, Pallas kernels for 0%

profile of v1, /device:TPU:0, one launch (start us, length us, event | category | flops | bytes accessed | tf_op | source)
XLA Modules:
  0.0 255.2 jit_solution(285584545406944324)
XLA Ops:
  6.5 1.7 pad_maximum_fusion
  8.3 0.7 broadcast_multiply_fusion
  9.2 30.4 %all-gather.4.cloned.1.call-done = bf16[256,2048]{1,0:T(8,128)(2,1)} async-done(((bf16[64,2048]{1,0:T(8,128)(2,1)}), bf16[256,2048]{1,0:T(8,128)(2,1)}) %all-gather.4.cloned.1.call-update) | async-done | bytes 1048592 | tf_op jit(solution)/shard_map/all_gather | solution.py:68
  39.6 1.2 fusion.32
  41.1 1.2 fusion.33
  42.3 0.2 fusion.7
  42.6 1.2 fusion.34
  43.8 0.2 fusion.5
  44.1 1.4 fusion.16
  45.5 1.3 fusion.15
  46.8 2.3 convolution_convert_fusion
  49.1 0.6 dynamic-slice
  49.8 33.6 %all-reduce.3.cloned.1.call-done = bf16[4,4,16,1536]{3,2,1,0:T(8,128)(2,1)} async-done(((bf16[4,4,16,1536]{3,2,1,0:T(8,128)(2,1)}), bf16[4,4,16,1536]{3,2,1,0:T(8,128)(2,1)}) %all-reduce.3.cloned.1.call-update) | async-done | bytes 786448
  83.4 2.3 dynamic-slice_bitcast_fusion
  85.7 4.6 %all-to-all-start = ((bf16[4,16,1536]{2,1,0:T(8,128)(2,1)}), bf16[4,16,1536]{2,1,0:T(8,128)(2,1)S(1)}, u32[]{:S(2)}, u32[]{:S(2)}) async-start(bf16[4,16,1536]{2,1,0:T(8,128)(2,1)} %dynamic-slice_bitcast_fusion), calls=%async_computation | async-start | bytes 393216 | tf_op jit(solution)/shard_map/all_to_all | solution.py:74
  90.3 6.4 %all-to-all-done = bf16[4,16,1536]{2,1,0:T(8,128)(2,1)S(1)} async-done(((bf16[4,16,1536]{2,1,0:T(8,128)(2,1)}), bf16[4,16,1536]{2,1,0:T(8,128)(2,1)S(1)}, u32[]{:S(2)}, u32[]{:S(2)}) %all-to-all-start) | async-done | bytes 196640 | tf_op jit(solution)/shard_map/all_to_all | solution.py:74
  96.8 0.2 fusion.26
  97.0 0.8 fusion.28
  98.0 19.4 %all-gather = f32[16,16,4]{1,2,0:T(4,128)S(1)} all-gather(f32[1,16,4]{1,2,0:T(4,128)S(1)} %add_bitcast_fusion), channel_id=1, replica_groups=mesh['grp'=2,'ctx'=4,'exp'=2,'tp'=2] {'ctx','exp','tp'}, dimensions={0}, use_global_device_ids=true | all-gather | bytes 4352 | tf_op jit(solution)/shard_map/all_gather | solution.py:64
  117.4 24.7 %all-gather.6.cloned.1.call-done = bf16[256,6144]{1,0:T(8,128)(2,1)} async-done(((bf16[16,6144]{1,0:T(8,128)(2,1)}), bf16[256,6144]{1,0:T(8,128)(2,1)}) %all-gather.6.cloned.1.call-update) | async-done | bytes 3145744 | tf_op jit(solution)/shard_map/all_gather | solution.py:84
  142.1 16.9 %fusion.3 = f32[256,2,1024]{2,0,1:T(8,128)} fusion(bf16[2,6144,1024]{2,1,0:T(8,128)(2,1)} %param.21, bf16[256,6144]{1,0:T(8,128)(2,1)} %all-gather.6.cloned.1.call-done), kind=kOutput, calls=%fused_computation.4 | convolution fusion | flops 6442450944 | bytes 30408704 | tf_op jit(solution)/shard_map/rd,edf->erf/dot_general | solution.py:87
  159.0 22.8 %fusion = bf16[256,6144]{1,0:T(8,128)(2,1)} fusion(bf16[2,1024,6144]{2,1,0:T(8,128)(2,1)} %param.23, f32[256,2,1024]{2,0,1:T(8,128)} %fusion.3, bf16[2,6144,1024]{2,1,0:T(8,128)(2,1)} %param.22, bf16[256,6144]{1,0:T(8,128)(2,1)S(1)} %copy-done.4, f32[256,2]{0,1:T(2,128)S(1)} %constant_dynamic-slice_fusion), kind=kOutput, calls=%fused_computation.1 | convolution fusion | flops 12890144768 | bytes 58722304 | tf_op jit(solution)/shard_map/dot_general | solution.py:92
  181.9 65.2 %reduce-scatter.5.cloned.1.call-done = bf16[16,6144]{1,0:T(8,128)(2,1)} async-done(((bf16[256,6144]{1,0:T(8,128)(2,1)}), bf16[16,6144]{1,0:T(8,128)(2,1)}) %reduce-scatter.5.cloned.1.call-update) | async-done | bytes 196624 | tf_op jit(solution)/shard_map/reduce_scatter | solution.py:93
  247.1 1.6 fusion.29
  (40 shorter events, 1.0 us)
Async XLA Ops:
  6.5 33.1 %all-gather.4.cloned.1.call-start = ((), (), s32[]{:S(2)}) async-start(), calls=%async_computation.2 | async-start | bytes 1310720 | tf_op jit(solution)/shard_map/all_gather | solution.py:68
  8.3 75.1 %all-reduce.3.cloned.1.call-start = ((), (), s32[]{:S(2)}) async-start(), calls=%async_computation.5 | async-start | bytes 1572864
  43.8 2.9 %slice-start = ((s8[4718592]{0:T(1024)(128)(4,1)}), s8[4194304]{0:T(1024)(128)(4,1)S(1)}, s32[]{:S(2)}) async-start(s8[4718592]{0:T(1024)(128)(4,1)} %bitcast.89), calls=%async_computation.6 | async-start | bytes 8388608
  44.0 2.7 %slice-start.1 = ((s8[4718592]{0:T(1024)(128)(4,1)}), s8[524288]{0:T(1024)(128)(4,1)S(1)}, s32[]{:S(2)}) async-start(s8[4718592]{0:T(1024)(128)(4,1)} %bitcast.89), calls=%async_computation.7 | async-start | bytes 1048576
  46.8 2.4 copy-start.5
  46.8 43.5 %copy-start.1 = (bf16[6144]{0:T(1024)(128)(2,1)S(1)}, bf16[6144]{0:T(1024)(128)(2,1)}, u32[]{:S(2)}) copy-start(bf16[6144]{0:T(1024)(128)(2,1)} %param.18) | copy-start | bytes 36868
  49.1 47.7 %copy-start = (bf16[16,6144]{1,0:T(8,128)(2,1)S(1)}, bf16[16,6144]{1,0:T(8,128)(2,1)}, u32[]{:S(2)}) copy-start(bf16[16,6144]{1,0:T(8,128)(2,1)} %param.16) | copy-start | bytes 589828
  49.1 48.8 %copy-start.2 = (s32[16,2]{0,1:T(2,128)S(1)}, s32[16,2]{0,1:T(2,128)}, u32[]{:S(2)}) copy-start(s32[16,2]{0,1:T(2,128)} %param.19) | copy-start | bytes 388
  49.1 48.8 %copy-start.3 = (f32[16,2]{0,1:T(2,128)S(1)}, f32[16,2]{0,1:T(2,128)}, u32[]{:S(2)}) copy-start(f32[16,2]{0,1:T(2,128)} %param.20) | copy-start | bytes 388
  85.7 11.1 %all-to-all-start = ((bf16[4,16,1536]{2,1,0:T(8,128)(2,1)}), bf16[4,16,1536]{2,1,0:T(8,128)(2,1)S(1)}, u32[]{:S(2)}, u32[]{:S(2)}) async-start(bf16[4,16,1536]{2,1,0:T(8,128)(2,1)} %dynamic-slice_bitcast_fusion), calls=%async_computation | async-start | bytes 393216 | tf_op jit(solution)/shard_map/all_to_all | solution.py:74
  90.3 51.8 %all-gather.6.cloned.1.call-start = ((), (), s32[]{:S(2)}) async-start(), calls=%async_computation.3 | async-start | bytes 3342336 | tf_op jit(solution)/shard_map/all_gather | solution.py:84
  97.8 149.2 %reduce-scatter.5.cloned.1.call-start = ((), (), s32[]{:S(2)}) async-start(), calls=%async_computation.4 | async-start | bytes 3342336 | tf_op jit(solution)/shard_map/reduce_scatter | solution.py:93
  142.1 16.9 %copy-start.4 = (bf16[256,6144]{1,0:T(8,128)(2,1)S(1)}, bf16[256,6144]{1,0:T(8,128)(2,1)}, u32[]{:S(2)}) copy-start(bf16[256,6144]{1,0:T(8,128)(2,1)} %all-gather.6.cloned.1.call-done) | copy-start | bytes 9437188
Sparse Core Ops, SparseCore 0:
  8.9 30.6 all-gather.3
  49.2 34.0 all-reduce.2
  98.0 44.0 all-gather.5
  182.0 65.0 reduce-scatter.4

commit v2 on v1

--- a/solution.py
+++ b/solution.py
@@ -1,8 +1,11 @@
+import functools
 import math
 
 import jax
 import jax.numpy as jnp
 from jax import lax
+from jax.experimental import pallas as pl
+from jax.experimental.pallas import tpu as pltpu
 from jax.sharding import PartitionSpec as P
 
 HEAD_SIZE = 128
@@ -38,6 +41,180 @@
     return jnp.concatenate(heads, axis=1)
 
 
+MESH = pl.DeviceIdType.MESH
+LANES = 128
+VMEM_LIMIT = 48 * 1024 * 1024
+
+
+def remote(src, dst, send_sem, recv_sem, device):
+    return pltpu.make_async_remote_copy(
+        src_ref=src, dst_ref=dst, send_sem=send_sem, recv_sem=recv_sem, device_id=device, device_id_type=MESH
+    )
+
+
+def greet(devices):
+    barrier = pltpu.get_barrier_semaphore()
+    for device in devices:
+        pl.semaphore_signal(barrier, inc=1, device_id=device, device_id_type=MESH)
+    pl.semaphore_wait(barrier, len(devices))
+
+
+def swap_kernel(ctx, exp, tp, part, gates, projected, all_gates, got, got_gates, sends, recvs, gate_sends, gate_recvs):
+    count = ctx * exp * tp
+    me = (lax.axis_index("ctx") * exp + lax.axis_index("exp")) * tp + lax.axis_index("tp")
+    peers, devices = [], []
+    for offset in range(1, count):
+        peer = lax.rem(me + offset, count)
+        peers.append(peer)
+        devices.append(
+            {"ctx": lax.div(peer, exp * tp), "exp": lax.rem(lax.div(peer, tp), exp), "tp": lax.rem(peer, tp)}
+        )
+    greet(devices)
+    copies = []
+    for i, (peer, device) in enumerate(zip(peers, devices)):
+        copies.append(remote(part.at[peer], got.at[me], sends.at[i], recvs.at[i], device))
+        copies[-1].start()
+    gate_copies = []
+    for i, device in enumerate(devices):
+        gate_copies.append(remote(gates, got_gates.at[me], gate_sends.at[i], gate_recvs.at[i], device))
+        gate_copies[-1].start()
+    got[me] = part[me]
+    got_gates[me] = gates[...]
+    for copy in copies + gate_copies:
+        copy.wait()
+    columns = part.shape[2]
+    for c in range(ctx):
+        total = got[c * exp * tp].astype(jnp.float32)
+        for j in range(1, exp * tp):
+            total += got[c * exp * tp + j].astype(jnp.float32)
+        projected[:, c * columns : (c + 1) * columns] = total
+    all_gates[...] = got_gates[...]
+
+
+def swap(part, gates, ctx, exp, tp):
+    count, tok_rows, columns = part.shape
+    whole = pl.BlockSpec(memory_space=pltpu.VMEM)
+    return pl.pallas_call(
+        functools.partial(swap_kernel, ctx, exp, tp),
+        out_shape=[
+            jax.ShapeDtypeStruct((tok_rows, ctx * columns), jnp.float32),
+            jax.ShapeDtypeStruct((count, tok_rows, LANES), jnp.float32),
+        ],
+        in_specs=[whole] * 2,
+        out_specs=[whole] * 2,
+        scratch_shapes=[
+            pltpu.VMEM((count, tok_rows, columns), jnp.bfloat16),
+            pltpu.VMEM((count, tok_rows, LANES), jnp.float32),
+        ]
+        + [pltpu.SemaphoreType.DMA((count - 1,))] * 4,
+        compiler_params=pltpu.CompilerParams(
+            collective_id=0, has_side_effects=True, vmem_limit_bytes=VMEM_LIMIT
+        ),
+    )(part, gates)
+
+
+def reduce_kernel(ctx, exp, tp, sums, out, got1, acc1, got2, acc2, got3, s1, v1, s2, v2, s3, v3):
+    c, e, t = lax.axis_index("ctx"), lax.axis_index("exp"), lax.axis_index("tp")
+    pair = lax.rem(t + 1, tp)
+    cs = [lax.rem(c + k, ctx) for k in range(ctx)]
+    es = [lax.rem(e + k, exp) for k in range(exp)]
+
+    def device(cc, ee, tt):
+        return {"ctx": cc, "exp": ee, "tp": tt}
+
+    greet(
+        [device(c, e, pair)]
+        + [device(c, es[j], t) for j in range(1, exp)]
+        + [device(cs[k], e, t) for k in range(1, ctx)]
+    )
+    order = list(range(1, ctx)) + [0]
+    first, second, third = {}, {}, {}
+    for j in list(range(1, exp)) + [0]:
+        for k in order:
+            first[k, j] = remote(
+                sums.at[cs[k], es[j], pair], got1.at[k, j], s1.at[k, j], v1.at[k, j], device(c, e, pair)
+            )
+            first[k, j].start()
+    for k in order:
+        for j in range(1, exp):
+            first[k, j].wait_recv()
+            acc1[j - 1, k] = (
+                sums[cs[k], es[j], t].astype(jnp.float32) + got1[k, j].astype(jnp.float32)
+            ).astype(jnp.bfloat16)
+            second[k, j] = remote(
+                acc1.at[j - 1, k], got2.at[j - 1, k], s2.at[j - 1, k], v2.at[j - 1, k], device(c, es[j], t)
+            )
+            second[k, j].start()
+    for k in order:
+        first[k, 0].wait_recv()
+        total = sums[cs[k], e, t].astype(jnp.float32) + got1[k, 0].astype(jnp.float32)
+        for j in range(1, exp):
+            second[k, j].wait_recv()
+            total += got2[j - 1, k].astype(jnp.float32)
+        if k > 0:
+            acc2[k - 1] = total.astype(jnp.bfloat16)
+            third[k] = remote(
+                acc2.at[k - 1], got3.at[k - 1], s3.at[k - 1], v3.at[k - 1], device(cs[k], e, t)
+            )
+            third[k].start()
+        else:
+            out[...] = total
+    for k in range(1, ctx):
+        third[k].wait_recv()
+        out[...] += got3[k - 1].astype(jnp.float32)
+    for copy in list(first.values()) + list(second.values()) + list(third.values()):
+        copy.wait_send()
+
+
+def reduce_rows(sums):
+    ctx, exp, tp, tok_rows, width = sums.shape
+    whole = pl.BlockSpec(memory_space=pltpu.VMEM)
+    block = (tok_rows, width)
+    return pl.pallas_call(
+        functools.partial(reduce_kernel, ctx, exp, tp),
+        out_shape=jax.ShapeDtypeStruct(block, jnp.float32),
+        in_specs=[whole],
+        out_specs=whole,
+        scratch_shapes=[
+            pltpu.VMEM((ctx, exp) + block, jnp.bfloat16),
+            pltpu.VMEM((exp - 1, ctx) + block, jnp.bfloat16),
+            pltpu.VMEM((exp - 1, ctx) + block, jnp.bfloat16),
+            pltpu.VMEM((ctx - 1,) + block, jnp.bfloat16),
+            pltpu.VMEM((ctx - 1,) + block, jnp.bfloat16),
+            pltpu.SemaphoreType.DMA((ctx, exp)),
+            pltpu.SemaphoreType.DMA((ctx, exp)),
+            pltpu.SemaphoreType.DMA((exp - 1, ctx)),
+            pltpu.SemaphoreType.DMA((exp - 1, ctx)),
+            pltpu.SemaphoreType.DMA((ctx - 1,)),
+            pltpu.SemaphoreType.DMA((ctx - 1,)),
+        ],
+        compiler_params=pltpu.CompilerParams(
+            collective_id=1, has_side_effects=True, vmem_limit_bytes=VMEM_LIMIT
+        ),
+    )(sums)
+
+
+def down_kernel(active, weights, out):
+    out[...] = jnp.dot(active[...], weights[...], preferred_element_type=jnp.float32).astype(jnp.bfloat16)
+
+
+def down(active, weights):
+    rows, hidden = active.shape
+    width = weights.shape[1]
+    tile = 512
+    return pl.pallas_call(
+        down_kernel,
+        grid=(width // tile,),
+        out_shape=jax.ShapeDtypeStruct((rows, width), jnp.bfloat16),
+        in_specs=[
+            pl.BlockSpec((rows, hidden), lambda i: (0, 0)),
+            pl.BlockSpec((hidden, tile), lambda i: (0, i)),
+        ],
+        out_specs=pl.BlockSpec((rows, tile), lambda i: (0, i)),
+        compiler_params=pltpu.CompilerParams(vmem_limit_bytes=VMEM_LIMIT),
+    )(active, weights)
+
+
 def shards(
     queries,
     rotated_key_heads,
@@ -61,18 +238,20 @@
     second = jax.nn.sigmoid(gate_logits[:, 1] - gate_logits[:, 0])
     names = jnp.arange(EXPERTS, dtype=jnp.int32)[None, :]
     row_gates = first[:, None] * (expert_ids[:, :1] == names) + second[:, None] * (expert_ids[:, 1:] == names)
-    gates = lax.all_gather(row_gates, all_axes, axis=0, tiled=True)
 
     qw, kw = queries.shape[1], rotated_key_heads.shape[1]
     own = jnp.concatenate([queries, rotated_key_heads, stored_value_heads], axis=1)
     qkv = lax.all_gather(own, "ctx", axis=0, tiled=True)
     attended = attend(qkv[:, :qw], qkv[:, qw : qw + kw], qkv[:, qw + kw :], block_order)
     part = jnp.dot(attended, out_weight, preferred_element_type=jnp.float32).astype(jnp.bfloat16)
-    part = part.reshape(ctx, exp * tp, tok_rows, -1)
-    part = lax.psum_scatter(part, ("exp", "tp"), scatter_dimension=1, tiled=True)
-    part = part.reshape(ctx, tok_rows, -1)
-    part = lax.all_to_all(part, "ctx", split_axis=0, concat_axis=0, tiled=True)
-    projected = jnp.transpose(part, (1, 0, 2)).reshape(tok_rows, width).astype(jnp.float32)
+    projected, gates = swap(
+        part.reshape(ctx * exp * tp, tok_rows, -1),
+        jnp.pad(row_gates, ((0, 0), (0, LANES - EXPERTS))),
+        ctx,
+        exp,
+        tp,
+    )
+    gates = gates.reshape(-1, LANES)
     hidden_state = (residual.astype(jnp.float32) + projected).astype(jnp.bfloat16)
     state = hidden_state.astype(jnp.float32)
     normed = (
@@ -83,15 +262,14 @@
 
     rows = lax.all_gather(normed, all_axes, axis=0, tiled=True)
     base = lax.axis_index("exp") * local_experts
-    actives = []
     gate_val = jnp.einsum("rd,edf->erf", rows, w_gate, preferred_element_type=jnp.float32)
     up_val = jnp.einsum("rd,edf->erf", rows, w_up, preferred_element_type=jnp.float32)
     local_gates = lax.dynamic_slice_in_dim(gates, base, local_experts, axis=1)
     active = (jax.nn.silu(gate_val) * up_val * local_gates.T[:, :, None]).astype(jnp.bfloat16)
     active = jnp.transpose(active, (1, 0, 2)).reshape(rows.shape[0], -1)
-    sums = jnp.dot(active, w_down.reshape(-1, width), preferred_element_type=jnp.float32)
-    mixture = lax.psum_scatter(sums.astype(jnp.bfloat16), all_axes, scatter_dimension=0, tiled=True)
-    return (state + mixture.astype(jnp.float32)).astype(jnp.bfloat16)
+    sums = down(active, w_down.reshape(-1, width))
+    mixture = reduce_rows(sums.reshape(ctx, exp, tp, tok_rows, width))
+    return (state + mixture).astype(jnp.bfloat16)
 
 
 def solution(mesh):

time: 256 us -> 199 us (0.78)
  waiting for transfers between devices: 160 us -> 73.2 us
  Pallas kernels: 0 us -> 68.6 us
  blocking collectives: 19.4 us -> 0 us
  matrix products: 47.2 us -> 34.1 us
  starting transfers between devices: 4.69 us -> 0.04 us
    pallas_call x0 -> x3, Pallas kernels: none -> 68.6 us  [the longest x1 28.4 us: reduce_rows(): pl.pallas_call(functools.partial(reduce_kernel, ctx, exp, tp), out_shape=...]
    reduce_scatter x1 -> x0, waiting for transfers between devices: 65.2 us -> none  [shards(): lax.psum_scatter(sums.astype(jnp.bfloat16), all_axes, scatter_dimension=0...]
    unnamed x5 -> x2, waiting for transfers between devices: 33.7 us -> 0.03 us
    all_gather x1, waiting for transfers between devices: 24.7 us -> 45.2 us  [shards(): rows = lax.all_gather(normed, all_axes, axis=0, tiled=True)]
    all_gather x1 -> x0, blocking collectives: 19.4 us -> none  [shards(): gates = lax.all_gather(row_gates, all_axes, axis=0, tiled=True)]
    dot_general x1, matrix products: 22.8 us -> 11.7 us  [shards(): jnp.einsum('rd,edf->erf', rows, w_up, preferred_element_type=jnp.float32)]
    all_to_all x1 -> x0, waiting for transfers between devices: 6.44 us -> none  [shards(): part = lax.all_to_all(part, 'ctx', split_axis=0, concat_axis=0, tiled=True)]
    all_to_all x1 -> x0, starting transfers between devices: 4.6 us -> none  [shards(): part = lax.all_to_all(part, 'ctx', split_axis=0, concat_axis=0, tiled=True)]
  transfers between devices with their start and end apart: 5 -> 2, of which waited for: 5 -> 2; matrix products, arithmetic and copies ran while one was open for 1% -> 2% of each run, Pallas kernels for 0% -> 0%
where the time goes in v2:
time: 199 us; the launch traced here: 198 us
  waiting for transfers between devices  73.2 us (37%)
  Pallas kernels  68.6 us (34%)
  matrix products  34.1 us (17%)
  between operations  13.6 us (7%)
  other arithmetic  6.24 us (3%)
  local copies, waits for them, and re-layouts  2.62 us (1%)
    all_gather x1, waiting for transfers between devices, shards(): rows = lax.all_gather(normed, all_axes, axis=0, tiled=True)  45.2 us
    pallas_call x1, Pallas kernels, reduce_rows(): pl.pallas_call(functools.partial(reduce_kernel, ctx, exp, tp), out_shape=...  28.4 us
    all_gather x1, waiting for transfers between devices, shards(): qkv = lax.all_gather(own, 'ctx', axis=0, tiled=True)  28 us
    pallas_call x1, Pallas kernels, swap(): pl.pallas_call(functools.partial(swap_kernel, ctx, exp, tp), out_shape=[j...  24.8 us
    dot_general x1, matrix products, shards(): jnp.einsum('rd,edf->erf', rows, w_gate, preferred_element_type=jnp.float32)  15.9 us
    pallas_call x1, Pallas kernels, down(): pl.pallas_call(down_kernel, grid=(width // tile,), out_shape=jax.ShapeDty...  15.3 us
    dot_general x1, matrix products, shards(): jnp.einsum('rd,edf->erf', rows, w_up, preferred_element_type=jnp.float32)  11.7 us
  transfers between devices with their start and end apart: 2, of which 2 were waited for; matrix products, arithmetic and copies ran while one was open for 2% of the time, Pallas kernels for 0%

profile of v2, /device:TPU:0, one launch (start us, length us, event | category | flops | bytes accessed | tf_op | source)
XLA Modules:
  0.0 198.4 jit_solution(3864231500044183954)
XLA Ops:
  6.5 1.7 pad_maximum_fusion
  8.3 0.7 broadcast_multiply_fusion
  9.1 0.7 convert_element_type.51
  9.8 0.8 slice_bitcast_fusion.9
  10.6 0.8 divide_bitcast_fusion.1
  11.5 28.0 %all-gather.3.cloned.1.call-done = bf16[256,2048]{1,0:T(8,128)(2,1)} async-done(((bf16[64,2048]{1,0:T(8,128)(2,1)}), bf16[256,2048]{1,0:T(8,128)(2,1)}) %all-gather.3.cloned.1.call-update) | async-done | bytes 1048592 | tf_op jit(solution)/shard_map/all_gather | solution.py:244
  39.6 1.2 fusion.29
  40.8 0.2 copy.20
  41.1 1.2 fusion.30
  42.3 0.2 fusion.6
  42.6 1.2 fusion.31
  43.8 0.2 fusion.4
  44.1 1.4 fusion.16
  45.5 1.3 fusion.15
  46.8 1.4 convolution_convert_fusion
  48.2 24.8 %shard_map.118 = (f32[16,6144]{1,0:T(8,128)S(1)}, f32[16,16,128]{2,1,0:T(8,128)S(1)}) custom-call(bf16[16,16,1536]{2,1,0:T(8,128)(2,1)S(1)} %bitcast.69, f32[16,128]{1,0:T(8,128)S(1)} %pad.4.gates), custom_call_target="tpu_custom_call" | custom-call | tf_op jit(solution)/shard_map/pallas_call | solution.py:97
  73.0 0.2 fusion.24
  73.2 0.8 fusion.26
  74.2 45.2 %all-gather.5.cloned.1.call-done = bf16[256,6144]{1,0:T(8,128)(2,1)} async-done(((bf16[16,6144]{1,0:T(8,128)(2,1)}), bf16[256,6144]{1,0:T(8,128)(2,1)}) %all-gather.5.cloned.1.call-update) | async-done | bytes 3145744 | tf_op jit(solution)/shard_map/all_gather | solution.py:263
  119.3 15.9 %fusion.2 = f32[256,2,1024]{2,0,1:T(8,128)S(1)} fusion(bf16[2,6144,1024]{2,1,0:T(8,128)(2,1)} %param.21, bf16[256,6144]{1,0:T(8,128)(2,1)} %all-gather.5.cloned.1.call-done), kind=kOutput, calls=%fused_computation.2 | convolution fusion | flops 6442450944 | bytes 30408704 | tf_op jit(solution)/shard_map/rd,edf->erf/dot_general | solution.py:265
  135.3 11.7 %fusion.10 = bf16[2,32,8,1024]{3,2,1,0:T(8,128)(2,1)S(1)} fusion(bf16[2,6144,1024]{2,1,0:T(8,128)(2,1)} %param.22, bf16[256,6144]{1,0:T(8,128)(2,1)S(1)} %copy-done.1, f32[256,2,1024]{2,0,1:T(8,128)S(1)} %fusion.2, f32[256,2]{0,1:T(2,128)S(1)} %copy.28), kind=kOutput, calls=%fused_computation.14 | convolution fusion | flops 6446120960 | bytes 31459328 | tf_op jit(solution)/shard_map/rd,edf->erf/dot_general | solution.py:266
  147.0 15.3 %shard_map.119 = bf16[256,6144]{1,0:T(8,128)(2,1)S(1)} custom-call(bf16[256,2048]{1,0:T(8,128)(2,1)S(1)} %bitcast.68, bf16[2048,6144]{1,0:T(8,128)(2,1)} %bitcast.71), custom_call_target="tpu_custom_call" | custom-call | tf_op jit(solution)/shard_map/pallas_call | solution.py:205
  162.4 28.4 %shard_map.120 = f32[16,6144]{1,0:T(8,128)S(1)} custom-call(bf16[4,2,2,16,6144]{4,3,2,1,0:T(8,128)(2,1)S(1)} %bitcast.67), custom_call_target="tpu_custom_call" | custom-call | tf_op jit(solution)/shard_map/pallas_call | solution.py:173
  190.9 0.7 fusion.27
  (23 shorter events, 0.9 us)
Async XLA Ops:
  6.5 33.1 %all-gather.3.cloned.1.call-start = ((), (), s32[]{:S(2)}) async-start(), calls=%async_computation | async-start | bytes 1310720 | tf_op jit(solution)/shard_map/all_gather | solution.py:244
  8.2 111.1 %all-gather.5.cloned.1.call-start = ((), (), s32[]{:S(2)}) async-start(), calls=%async_computation.1 | async-start | bytes 3342336 | tf_op jit(solution)/shard_map/all_gather | solution.py:263
  43.8 2.9 %slice-start = ((s8[4718592]{0:T(1024)(128)(4,1)}), s8[4194304]{0:T(1024)(128)(4,1)S(1)}, s32[]{:S(2)}) async-start(s8[4718592]{0:T(1024)(128)(4,1)} %bitcast.76), calls=%async_computation.2 | async-start | bytes 8388608
  44.0 2.7 %slice-start.1 = ((s8[4718592]{0:T(1024)(128)(4,1)}), s8[524288]{0:T(1024)(128)(4,1)S(1)}, s32[]{:S(2)}) async-start(s8[4718592]{0:T(1024)(128)(4,1)} %bitcast.76), calls=%async_computation.3 | async-start | bytes 1048576
  46.8 26.2 %copy-start = (bf16[16,6144]{1,0:T(8,128)(2,1)S(1)}, bf16[16,6144]{1,0:T(8,128)(2,1)}, u32[]{:S(2)}) copy-start(bf16[16,6144]{1,0:T(8,128)(2,1)} %param.16) | copy-start | bytes 589828
  119.3 15.9 %copy-start.1 = (bf16[256,6144]{1,0:T(8,128)(2,1)S(1)}, bf16[256,6144]{1,0:T(8,128)(2,1)}, u32[]{:S(2)}) copy-start(bf16[256,6144]{1,0:T(8,128)(2,1)} %all-gather.5.cloned.1.call-done) | copy-start | bytes 9437188
Sparse Core Ops, SparseCore 0:
  8.9 30.6 all-gather.2
  74.1 45.1 all-gather.4

commit v3 on v2

--- a/solution.py
+++ b/solution.py
@@ -194,6 +194,61 @@
     )(sums)
 
 
+def gather_kernel(ctx, exp, tp, own, out, s1, v1, s2, v2, s3, v3):
+    c, e, t = lax.axis_index("ctx"), lax.axis_index("exp"), lax.axis_index("tp")
+    pair = lax.rem(t + 1, tp)
+    to_c = [lax.rem(c + k, ctx) for k in range(ctx)]
+    from_c = [lax.rem(c + ctx - k, ctx) for k in range(ctx)]
+    to_e = [lax.rem(e + j, exp) for j in range(exp)]
+    from_e = [lax.rem(e + exp - j, exp) for j in range(exp)]
+    near = {"ctx": c, "exp": e, "tp": pair}
+    rows = [{"ctx": to_c[k], "exp": e, "tp": t} for k in range(1, ctx)]
+    sides = [{"ctx": c, "exp": to_e[j], "tp": t} for j in range(1, exp)]
+    greet([near] + rows + sides)
+    out[c, e, t] = own[...]
+    copies, first, second = [], {}, {}
+
+    def send(cc, ee, send_sem, recv_sem, device):
+        block = out.at[cc, ee, t]
+        copy = remote(block, block, send_sem, recv_sem, device)
+        copy.start()
+        copies.append(copy)
+        return copy
+
+    for k in range(1, ctx):
+        first[k] = send(c, e, s1.at[k - 1], v1.at[k - 1], rows[k - 1])
+    third = []
+    for k in range(ctx):
+        if k > 0:
+            first[k].wait_recv()
+        for j in range(1, exp):
+            second[k, j] = send(from_c[k], e, s2.at[k, j - 1], v2.at[k, j - 1], sides[j - 1])
+        third.append(send(from_c[k], e, s3.at[k, 0], v3.at[k, 0], near))
+    for k in range(ctx):
+        for j in range(1, exp):
+            second[k, j].wait_recv()
+            third.append(send(from_c[k], from_e[j], s3.at[k, j], v3.at[k, j], near))
+    for copy in third:
+        copy.wait_recv()
+    for copy in copies:
+        copy.wait_send()
+
+
+def gather_rows(own, ctx, exp, tp):
+    whole = pl.BlockSpec(memory_space=pltpu.VMEM)
+    counts = [(ctx - 1,), (ctx, exp - 1), (ctx, exp)]
+    return pl.pallas_call(
+        functools.partial(gather_kernel, ctx, exp, tp),
+        out_shape=jax.ShapeDtypeStruct((ctx, exp, tp) + own.shape, own.dtype),
+        in_specs=[whole],
+        out_specs=whole,
+        scratch_shapes=[pltpu.SemaphoreType.DMA(n) for n in counts for _ in range(2)],
+        compiler_params=pltpu.CompilerParams(
+            collective_id=2, has_side_effects=True, vmem_limit_bytes=VMEM_LIMIT
+        ),
+    )(own)
+
+
 def down_kernel(active, weights, out):
     out[...] = jnp.dot(active[...], weights[...], preferred_element_type=jnp.float32).astype(jnp.bfloat16)
 
@@ -260,7 +315,7 @@
         * norm_gain.astype(jnp.float32)
     ).astype(jnp.bfloat16)
 
-    rows = lax.all_gather(normed, all_axes, axis=0, tiled=True)
+    rows = gather_rows(normed, ctx, exp, tp).reshape(-1, width)
     base = lax.axis_index("exp") * local_experts
     gate_val = jnp.einsum("rd,edf->erf", rows, w_gate, preferred_element_type=jnp.float32)
     up_val = jnp.einsum("rd,edf->erf", rows, w_up, preferred_element_type=jnp.float32)

time: 199 us -> 180 us (0.905)
  waiting for transfers between devices: 73.2 us -> 28.1 us
  Pallas kernels: 68.6 us -> 99.9 us
  matrix products: 34.1 us -> 29.7 us
    all_gather x1 -> x0, waiting for transfers between devices: 45.2 us -> none  [shards(): rows = lax.all_gather(normed, all_axes, axis=0, tiled=True)]
    pallas_call x0 -> x1, Pallas kernels: none -> 27.9 us  [gather_rows(): pl.pallas_call(functools.partial(gather_kernel, ctx, exp, tp), out_shape=...]
    dot_general x1, matrix products: 15.9 us -> 11.6 us  [shards(): jnp.einsum('rd,edf->erf', rows, w_gate, preferred_element_type=jnp.float32)]
    pallas_call x1, Pallas kernels: 28.4 us -> 31.8 us  [reduce_rows(): pl.pallas_call(functools.partial(reduce_kernel, ctx, exp, tp), out_shape=...]
  transfers between devices with their start and end apart: 2 -> 1, of which waited for: 2 -> 1; matrix products, arithmetic and copies ran while one was open for 2% -> 2% of each run, Pallas kernels for 0% -> 0%
where the time goes in v3:
time: 180 us; the launch traced here: 179 us
  Pallas kernels  99.9 us (56%)
  matrix products  29.7 us (16%)
  waiting for transfers between devices  28.1 us (16%)
  between operations  13.6 us (8%)
  other arithmetic  5.57 us (3%)
  local copies, waits for them, and re-layouts  2.62 us (1%)
    pallas_call x1, Pallas kernels, reduce_rows(): pl.pallas_call(functools.partial(reduce_kernel, ctx, exp, tp), out_shape=...  31.8 us
    all_gather x1, waiting for transfers between devices, shards(): qkv = lax.all_gather(own, 'ctx', axis=0, tiled=True)  28.1 us
    pallas_call x1, Pallas kernels, gather_rows(): pl.pallas_call(functools.partial(gather_kernel, ctx, exp, tp), out_shape=...  27.9 us
    pallas_call x1, Pallas kernels, swap(): pl.pallas_call(functools.partial(swap_kernel, ctx, exp, tp), out_shape=[j...  24.8 us
    pallas_call x1, Pallas kernels, down(): pl.pallas_call(down_kernel, grid=(width // tile,), out_shape=jax.ShapeDty...  15.3 us
    dot_general x1, matrix products, shards(): jnp.einsum('rd,edf->erf', rows, w_up, preferred_element_type=jnp.float32)  11.7 us
    dot_general x1, matrix products, shards(): jnp.einsum('rd,edf->erf', rows, w_gate, preferred_element_type=jnp.float32)  11.6 us
  transfers between devices with their start and end apart: 1, of which 1 were waited for; matrix products, arithmetic and copies ran while one was open for 2% of the time, Pallas kernels for 0%

profile of v3, /device:TPU:0, one launch (start us, length us, event | category | flops | bytes accessed | tf_op | source)
XLA Modules:
  0.0 179.5 jit_solution(8148289402154756817)
XLA Ops:
  6.5 1.7 pad_maximum_fusion
  8.3 0.7 broadcast_multiply_fusion
  9.1 0.7 convert_element_type.51
  9.8 0.8 slice_bitcast_fusion.9
  10.5 0.8 divide_bitcast_fusion.1
  11.5 28.1 %all-gather.2.cloned.1.call-done = bf16[256,2048]{1,0:T(8,128)(2,1)} async-done(((bf16[64,2048]{1,0:T(8,128)(2,1)}), bf16[256,2048]{1,0:T(8,128)(2,1)}) %all-gather.2.cloned.1.call-update) | async-done | bytes 1048592 | tf_op jit(solution)/shard_map/all_gather | solution.py:299
  39.6 1.2 fusion.21
  40.8 0.2 copy.20
  40.9 0.2 copy.24
  41.1 1.2 fusion.22
  42.3 0.2 fusion.2
  42.6 1.2 fusion.23
  43.8 0.2 fusion
  44.1 1.4 fusion.8
  45.5 1.3 fusion.7
  46.8 1.4 convolution_convert_fusion
  48.2 24.8 %shard_map.118 = (f32[16,6144]{1,0:T(8,128)S(1)}, f32[16,16,128]{2,1,0:T(8,128)S(1)}) custom-call(bf16[16,16,1536]{2,1,0:T(8,128)(2,1)S(1)} %bitcast.67, f32[16,128]{1,0:T(8,128)S(1)} %pad.4.gates), custom_call_target="tpu_custom_call" | custom-call | tf_op jit(solution)/shard_map/pallas_call | solution.py:97
  73.0 0.2 fusion.16
  73.5 27.9 %shard_map.119 = bf16[4,2,2,16,6144]{4,3,2,1,0:T(8,128)(2,1)S(1)} custom-call(bf16[16,6144]{1,0:T(8,128)(2,1)S(1)} %fusion.18.own), custom_call_target="tpu_custom_call" | custom-call | tf_op jit(solution)/shard_map/pallas_call | solution.py:240
  101.4 11.6 %fusion.24 = f32[256,2,1024]{2,0,1:T(8,128)S(1)} fusion(bf16[256,6144,1]{1,0,2:T(8,128)(2,1)S(1)} %bitcast.65, bf16[2,6144,1024]{2,1,0:T(8,128)(2,1)} %param.21), kind=kOutput, calls=%fused_computation.51 | convolution fusion | flops 6442450944 | bytes 30408704 | tf_op jit(solution)/shard_map/rd,edf->erf/dot_general | solution.py:320
  113.0 11.7 %fusion.4 = bf16[2,32,8,1024]{3,2,1,0:T(8,128)(2,1)S(1)} fusion(bf16[256,6144,1]{1,0,2:T(8,128)(2,1)S(1)} %bitcast.66, bf16[2,6144,1024]{2,1,0:T(8,128)(2,1)} %param.22, f32[256,2,1024]{2,0,1:T(8,128)S(1)} %fusion.24, f32[256,2]{0,1:T(2,128)S(1)} %copy.28), kind=kOutput, calls=%fused_computation.10 | convolution fusion | flops 6446120960 | bytes 31459328 | tf_op jit(solution)/shard_map/rd,edf->erf/dot_general | solution.py:321
  124.7 15.3 %shard_map.120 = bf16[256,6144]{1,0:T(8,128)(2,1)S(1)} custom-call(bf16[256,2048]{1,0:T(8,128)(2,1)S(1)} %bitcast.64, bf16[2048,6144]{1,0:T(8,128)(2,1)} %bitcast.69), custom_call_target="tpu_custom_call" | custom-call | tf_op jit(solution)/shard_map/pallas_call | solution.py:260
  140.1 31.8 %shard_map.121 = f32[16,6144]{1,0:T(8,128)S(1)} custom-call(bf16[4,2,2,16,6144]{4,3,2,1,0:T(8,128)(2,1)S(1)} %bitcast.63), custom_call_target="tpu_custom_call" | custom-call | tf_op jit(solution)/shard_map/pallas_call | solution.py:173
  171.9 0.7 fusion.19
  (19 shorter events, 0.8 us)
Async XLA Ops:
  6.5 33.1 %all-gather.2.cloned.1.call-start = ((), (), s32[]{:S(2)}) async-start(), calls=%async_computation | async-start | bytes 1310720 | tf_op jit(solution)/shard_map/all_gather | solution.py:299
  43.8 2.9 %slice-start = ((s8[4718592]{0:T(1024)(128)(4,1)}), s8[4194304]{0:T(1024)(128)(4,1)S(1)}, s32[]{:S(2)}) async-start(s8[4718592]{0:T(1024)(128)(4,1)} %bitcast.74), calls=%async_computation.1 | async-start | bytes 8388608
  44.0 2.7 %slice-start.1 = ((s8[4718592]{0:T(1024)(128)(4,1)}), s8[524288]{0:T(1024)(128)(4,1)S(1)}, s32[]{:S(2)}) async-start(s8[4718592]{0:T(1024)(128)(4,1)} %bitcast.74), calls=%async_computation.2 | async-start | bytes 1048576
  46.8 26.2 %copy-start = (bf16[16,6144]{1,0:T(8,128)(2,1)S(1)}, bf16[16,6144]{1,0:T(8,128)(2,1)}, u32[]{:S(2)}) copy-start(bf16[16,6144]{1,0:T(8,128)(2,1)} %param.16) | copy-start | bytes 589828
Sparse Core Ops, SparseCore 0:
  8.9 30.6 all-gather.1
